TPU v7x, 32 devices: a whole 2x2x4 slice. The times are simulated.
32 devices in a mesh: gx: 4 (over z), gy: 4 (over y, x), gz: 2 (over core).
Axes of the slice: x: 2, y: 2, z: 4, core: 2. Of those that a mesh axis runs over, the one named last changes fastest.
Arguments:
- mass_per_volume: float32 [16, 64, 512], P('gz', 'gx', 'gy'), may hold values from 0.5 to 2
- flow_speed: float32 [3, 16, 64, 512], P(None, 'gz', 'gx', 'gy'), may hold values from -3 to 3
- pressure: float32 [16, 64, 512], P('gz', 'gx', 'gy'), may hold values from 0.5 to 2
- cotangent: float32 [5, 16, 64, 512], P(None, 'gz', 'gx', 'gy'), may hold values from -6 to 6
- weight_inner: float32 [64, 9], replicated, may hold values from -2 to 2
- weight_middle: float32 [64, 64], replicated, may hold values from -0.75 to 0.75
- weight_outer: float32 [64], replicated, may hold values from -0.75 to 0.75
Outputs:
- state_next: float32 [5, 16, 64, 512], P(None, 'gz', 'gx', 'gy')
- adjoint_density: float32 [16, 64, 512], P('gz', 'gx', 'gy')
- adjoint_velocity: float32 [3, 16, 64, 512], P(None, 'gz', 'gx', 'gy')
- adjoint_pressure: float32 [16, 64, 512], P('gz', 'gx', 'gy')
- adjoint_inner: float32 [64, 9], replicated
- adjoint_middle: float32 [64, 64], replicated
- adjoint_outer: float32 [64], replicated
All inputs are finite; a program needn't handle non-finite values.
Results may differ from a plain program's by a relative error of at most 0.0003.
Values sent between devices are 32-bit elements; how exact they have to be, the bound alone decides.
A program may use at most 64 MiB of HBM per device.

v0:
```python
import functools
import math

import jax
import jax.numpy as jnp
import ml_dtypes
import numpy as np
from jax import lax
from jax.experimental import pallas as pl
from jax.experimental.pallas import tpu as pltpu
from jax.sharding import PartitionSpec as P

TIME_STEP = 0.1
ALPHA = 1.0 / 3.0
MESH = pl.DeviceIdType.MESH
F32 = jnp.float32
BF16 = jnp.bfloat16
ROOT = (-1.0 + math.sqrt(1.0 - 4.0 * ALPHA**2)) / (2.0 * ALPHA)
FIELDS = 9
HID = 64


def split_np(a):
    hi = a.astype(ml_dtypes.bfloat16)
    lo = (a - hi.astype(np.float64)).astype(ml_dtypes.bfloat16)
    return np.concatenate([hi, lo, hi], 1)


def split(x):
    hi = x.astype(BF16)
    lo = (x - hi.astype(F32)).astype(BF16)
    return hi, lo


def stack3(x):
    hi, lo = split(x)
    return jnp.concatenate([hi, hi, lo], 0)


def x_tables(xc, zc, groups):
    n = xc * groups
    r = ROOT
    c0 = 1.0 + 2.0 * ALPHA * r
    period = 1.0 - r**n
    gain = (7.0 / 9.0 * (r - 1 / r) + 1.0 / 36.0 * (r**2 - r**-2)) / c0
    fix = (1 / r - r) / 36.0 / c0
    i = np.arange(xc)
    d = i[:, None] - i[None, :]
    own = np.where(d == 0, 0.0, np.sign(d) * gain * r ** np.abs(d))
    own = own + np.where(np.abs(d) == 1, np.sign(d) * fix, 0.0)
    own = own + gain * (r ** (d + n) - r ** (n - d)) / period
    eye = np.eye(zc)
    last = np.zeros((1, xc))
    last[0, -1] = 1.0
    first = np.zeros((1, xc))
    first[0, 0] = 1.0
    right = (r ** (xc - 1 - i))[None]
    left = (r**i)[None]
    full = np.concatenate(
        [np.kron(eye, own)] + [np.kron(eye, row) for row in (last, right, left, first)], 0
    )
    add_last = np.zeros((xc, 1))
    add_last[0] = fix
    add_first = np.zeros((xc, 1))
    add_first[-1] = -fix
    add = np.concatenate(
        [
            np.kron(eye, column)
            for column in (
                add_last,
                (gain * r ** (i + 1))[:, None],
                (-gain * r ** (xc - i))[:, None],
                add_first,
            )
        ],
        1,
    )
    return split_np(full), split_np(add)


def kernel(
    dims, offsets, rho_ref, vel_ref, prs_ref, ct_ref, xfull_ref, xadd_ref, w1_ref, w2_ref, w2t_ref,
    b1_ref, w3_ref, next_ref, arho_ref, avel_ref, aprs_ref, wg_ref,
    f0, fx, fy, fz, der, back, w1s, w2s, w2ts, b1s, acc, w3acc,
    mom, momr, ypl, ypr, yl, yr, zlo, zhi, part_z, part_x, part_y, send_sem, recv_sem,
):
    gxn, gyn, gzn = dims
    sizes = {"gx": gxn, "gy": gyn, "gz": gzn}
    me = {axis: lax.axis_index(axis) for axis in sizes}
    lane = lax.broadcasted_iota(jnp.int32, (1, 1, 128), 2)

    def other(axis, offset):
        return {axis: lax.rem(me[axis] + (offset + sizes[axis]), sizes[axis])}

    barrier = pltpu.get_barrier_semaphore()
    total = 0
    for axis in sizes:
        for offset in range(1, sizes[axis]):
            pl.semaphore_signal(barrier, inc=1, device_id=other(axis, offset), device_id_type=MESH)
            total += 1

    used = [0]

    def remote(src, dst, axis, offset):
        k = used[0]
        used[0] += 1
        copy = pltpu.make_async_remote_copy(
            src_ref=src, dst_ref=dst, send_sem=send_sem.at[k], recv_sem=recv_sem.at[k],
            device_id=other(axis, offset), device_id_type=MESH,
        )
        copy.start()
        return copy

    pending = []

    def send_z(ph, src):
        a = remote(src.at[:, 10:16], zlo.at[ph], "gz", 1)
        b = remote(src.at[:, 0:6], zhi.at[ph], "gz", -1)
        return [a, b]

    def send_y(ph, src):
        for j in range(FIELDS):
            for q in range(4):
                block = src[j, 4 * q : 4 * q + 4]
                at = 32 * q + 3 * j
                inside = (lane >= at) & (lane < at + 3)
                hi_edge = pltpu.roll(block, (at - 125) % 128, 2)
                lo_edge = pltpu.roll(block, at, 2) if at else block
                if j == 0 and q == 0:
                    vl, vr = hi_edge, lo_edge
                    keep = [vl, vr]
                else:
                    keep = [
                        jnp.where(inside, hi_edge, keep[0]),
                        jnp.where(inside, lo_edge, keep[1]),
                    ]
        ypl[ph] = keep[0]
        ypr[ph] = keep[1]
        return [
            remote(ypl.at[ph], yl.at[ph], "gy", 1),
            remote(ypr.at[ph], yr.at[ph], "gy", -1),
        ]

    def send_x(ph, src, put):
        def one(j, carry):
            y = jnp.dot(
                xfull_ref[...], stack3(src[j].reshape(128, 128)), preferred_element_type=F32
            )
            put(j, y[:128].reshape(16, 8, 128))
            for m in range(4):
                mom[ph, m, j] = y[128 + 8 * m : 136 + 8 * m]
            return carry

        lax.fori_loop(0, FIELDS, one, 0, unroll=3)
        copies = []
        for slot, offset in enumerate(offsets):
            lo = 0 if offset == 1 else 1
            hi = 4 if offset == -1 else 3
            copies.append(
                remote(mom.at[ph, lo:hi], momr.at[ph, slot, lo:hi], "gx", offset)
            )
        return copies

    def dy(ph, src, j):
        outs = []
        for q in range(4):
            at = 32 * q + 3 * j
            f = src[j, 4 * q : 4 * q + 4]
            el = pltpu.roll(yl[ph], (125 - at) % 128, 2)
            er = pltpu.roll(yr[ph], (-at) % 128, 2) if at else yr[ph]

            def ahead(s):
                return pltpu.roll(jnp.where(lane < s, er, f), 128 - s, 2)

            def behind(s):
                return pltpu.roll(jnp.where(lane >= 128 - s, el, f), s, 2)

            outs.append(
                0.75 * (ahead(1) - behind(1))
                - 0.15 * (ahead(2) - behind(2))
                + (1.0 / 60.0) * (ahead(3) - behind(3))
            )
        return jnp.concatenate(outs, 0)

    def dz(ph, src, j):
        ext = jnp.concatenate([zlo[ph, j], src[j], zhi[ph, j]], 0)

        def shifted(s):
            return ext[6 + 2 * s : 22 + 2 * s]

        return (
            0.75 * (shifted(1) - shifted(-1))
            - 0.15 * (shifted(2) - shifted(-2))
            + (1.0 / 60.0) * (shifted(3) - shifted(-3))
        )

    period = 1.0 - ROOT ** (16 * gxn)

    def add_x(ph, add):
        def one(j, carry):
            va = jnp.zeros((8, 128), F32)
            vb = jnp.zeros((8, 128), F32)
            for slot, offset in enumerate(offsets):
                wa = ROOT ** (16 * (offset % gxn - 1)) / period
                wb = ROOT ** (16 * ((-offset) % gxn - 1)) / period
                va = va + wa * momr[ph, slot, 1, j]
                vb = vb + wb * momr[ph, slot, 2, j]
            rows = jnp.concatenate(
                [
                    momr[ph, offsets.index(1), 0, j],
                    va,
                    vb,
                    momr[ph, offsets.index(-1), 3, j],
                ],
                0,
            )
            y = jnp.dot(xadd_ref[...], stack3(rows), preferred_element_type=F32)
            add(j, y.reshape(16, 8, 128))
            return carry

        lax.fori_loop(0, FIELDS, one, 0, unroll=3)

    f0[0:3] = vel_ref[...]
    f0[3] = prs_ref[...] / rho_ref[...]
    f0[4:9] = ct_ref[...]
    pl.semaphore_wait(barrier, total)
    cz = send_z(0, f0)
    cy = send_y(0, f0)

    def put0(j, value):
        der[0, j] = value

    cx = send_x(0, f0, put0)
    pending += cz + cy + cx

    def halves(src, dst, third):
        x = src[...]
        hi, lo = split(x)
        col = lax.broadcasted_iota(jnp.int32, x.shape, 1)
        mid = (col >= third) & (col < 2 * third)
        dst[...] = jnp.where(mid, lo.astype(F32), hi.astype(F32)).astype(BF16)

    halves(w1_ref, w1s, 80)
    halves(w2_ref, w2s, HID)
    halves(w2t_ref, w2ts, HID)
    halves(b1_ref, b1s, 8 * HID)
    acc[...] = jnp.zeros_like(acc)
    w3acc[...] = jnp.zeros_like(w3acc)

    for c in cz:
        c.wait_recv()
    for j in range(FIELDS):
        der[2, j] = dz(0, f0, j)
    for c in cy:
        c.wait_recv()
    for j in range(FIELDS):
        der[1, j] = dy(0, f0, j)
    for c in cx:
        c.wait_recv()

    def add0(j, value):
        der[0, j] = der[0, j] + value

    add_x(0, add0)

    sub = lax.broadcasted_iota(jnp.int32, (8, 128), 0)

    def group(g, carry):
        feats = [der[k, i, g] for k in range(3) for i in range(3)]
        pre = jnp.dot(
            w1s[...],
            stack3(jnp.concatenate(feats + [jnp.zeros((8, 128), F32)], 0)),
            preferred_element_type=F32,
        )
        h1 = jnp.tanh(
            jnp.concatenate([pre[80 * x : 80 * x + 64] for x in range(8)], 1)
        )
        ft = jnp.concatenate([pre[80 * x + 64 : 80 * x + 80] for x in range(8)], 1)
        h1h, h1l = split(h1)
        h2 = jnp.tanh(
            jnp.dot(
                w2s[...], jnp.concatenate([h1h, h1h, h1l], 0), preferred_element_type=F32
            )
        )
        w3 = w3_ref[...]
        o = jnp.zeros((8, 128), F32)
        for x in range(8):
            row = jnp.sum(h2[:, 128 * x : 128 * x + 128] * w3, 0, keepdims=True)
            o = jnp.where(sub == x, row, o)
        decay = jnp.exp(-jnp.abs(o))
        eddy = 0.5 * (jnp.maximum(o, 0.0) + jnp.log1p(decay))
        sig = jnp.where(o >= 0.0, 1.0, decay) / (1.0 + decay)

        rho = rho_ref[g]
        prs = prs_ref[g]
        u = [vel_ref[i, g] for i in range(3)]
        ct = [ct_ref[i, g] for i in range(5)]
        q = u[0] * u[0] + u[1] * u[1] + u[2] * u[2]
        energy = prs / 0.4 + 0.5 * rho * q
        stag = energy + prs
        att = rho * eddy
        s = [[TIME_STEP * der[k, 4 + m, g] for m in range(5)] for k in range(3)]
        grad3 = [der[k, 3, g] for k in range(3)]
        flux_refs = (fx, fy, fz)
        att_bar = jnp.zeros((8, 128), F32)
        rho_bar = jnp.zeros((8, 128), F32)
        stag_bar = s[0][4] * u[0] + s[1][4] * u[1] + s[2][4] * u[2]
        for k in range(3):
            ref = flux_refs[k]
            mass = rho * u[k]
            ref[4, g] = mass
            inner = s[k][0]
            for i in range(3):
                value = mass * u[i] - att * feats[3 * k + i]
                if i == k:
                    value = value + prs
                ref[5 + i, g] = value
                att_bar = att_bar - s[k][1 + i] * feats[3 * k + i]
                inner = inner + s[k][1 + i] * u[i]
            ref[8, g] = stag * u[k] - 3.5 * att * grad3[k]
            ref[3, g] = -3.5 * att * s[k][4]
            att_bar = att_bar - 3.5 * s[k][4] * grad3[k]
            rho_bar = rho_bar + inner * u[k]
        for j in range(3):
            t = s[j][0] + ct[1 + j] + (stag_bar + ct[4]) * u[j]
            for i in range(3):
                t = t + (s[j][1 + i] + s[i][1 + j]) * u[i]
            avel_ref[j, g] = rho * t + stag * s[j][4]
        aprs_ref[g] = s[0][1] + s[1][2] + s[2][3] + stag_bar + (stag_bar + ct[4]) / 0.4
        arho_ref[g] = (
            rho_bar + 0.5 * q * (stag_bar + ct[4]) + att_bar * eddy + ct[0]
            + ct[1] * u[0] + ct[2] * u[1] + ct[3] * u[2]
        )
        next_ref[0, g] = rho
        for i in range(3):
            next_ref[1 + i, g] = rho * u[i]
        next_ref[4, g] = energy

        ob = 0.5 * att_bar * rho * sig
        seeds = []
        outer = w3acc[...]
        for x in range(8):
            row = jnp.broadcast_to(ob[x : x + 1], (HID, 128))
            seeds.append(row * w3)
            outer = outer + row * h2[:, 128 * x : 128 * x + 128]
        w3acc[...] = outer
        a2 = jnp.concatenate(seeds, 1) * (1.0 - h2 * h2)
        a2h, a2l = split(a2)
        a1 = jnp.dot(
            w2ts[...], jnp.concatenate([a2h, a2h, a2l], 0), preferred_element_type=F32
        ) * (1.0 - h1 * h1)
        a1h, a1l = split(a1)
        tall_h = jnp.concatenate([a1h[:, 128 * x : 128 * x + 128] for x in range(8)], 0)
        tall_l = jnp.concatenate([a1l[:, 128 * x : 128 * x + 128] for x in range(8)], 0)
        fbar = jnp.dot(
            b1s[...], jnp.concatenate([tall_h, tall_h, tall_l], 0), preferred_element_type=F32
        )
        for k in range(3):
            for i in range(3):
                c = 3 * k + i
                flux_refs[k][i, g] = fbar[8 * c : 8 * c + 8] - att * s[k][1 + i]
        fth, ftl = split(ft)
        acc[:, :160] = acc[:, :160] + lax.dot_general(
            jnp.concatenate([a2h, a2l, a1h, a1l], 0),
            jnp.concatenate([h1h, h1l, fth, ftl], 0),
            (((1,), (1,)), ((), ())),
            preferred_element_type=F32,
        )
        return carry

    lax.fori_loop(0, 16, group, 0)

    wlane = lax.broadcasted_iota(jnp.int32, (HID, 128), 1)
    mid_w = acc[0:64, 0:128] + acc[64:128, 0:128] + pltpu.roll(acc[0:64, 0:128], 64, 1)
    in_w = acc[128:192, 128:256] + acc[192:256, 128:256]
    in_w = in_w + pltpu.roll(acc[128:192, 128:256], 112, 1)
    in_w = pltpu.roll(in_w, 64, 1)
    out_w = jnp.sum(w3acc[...], 1, keepdims=True)
    mine = jnp.where(
        wlane < 64, mid_w, jnp.where(wlane < 80, in_w, jnp.where(wlane == 80, out_w, 0.0))
    )

    def exchange(buf, axis, value):
        buf[me[axis]] = value
        return [
            remote(buf.at[me[axis]], buf.at[me[axis]], axis, offset)
            for offset in range(1, sizes[axis])
        ]

    def total_of(buf, axis):
        value = buf[0]
        for i in range(1, sizes[axis]):
            value = value + buf[i]
        return value

    ez = exchange(part_z, "gz", mine)
    cz = send_z(1, fz)
    cy = send_y(1, fy)

    def put1(j, value):
        back[j] = value

    cx = send_x(1, fx, put1)
    for c in ez:
        c.wait_recv()
    ex = exchange(part_x, "gx", total_of(part_z, "gz"))
    for c in cz:
        c.wait_recv()
    for j in range(FIELDS):
        back[j] = back[j] + dz(1, fz, j)
    for c in cy:
        c.wait_recv()
    for j in range(FIELDS):
        back[j] = back[j] + dy(1, fy, j)
    for c in ex:
        c.wait_recv()
    ey = exchange(part_y, "gy", total_of(part_x, "gx"))
    for c in cx:
        c.wait_recv()

    def add1(j, value):
        back[j] = back[j] + value

    add_x(1, add1)
    for m in range(5):
        next_ref[m] = next_ref[m] - TIME_STEP * back[4 + m]
    for j in range(3):
        avel_ref[j] = avel_ref[j] - back[j]
    inv = 1.0 / rho_ref[...]
    heat = back[3] * inv
    aprs_ref[...] = aprs_ref[...] - heat
    arho_ref[...] = arho_ref[...] + heat * f0[3]
    for c in ey:
        c.wait_recv()
    cells = 16384 * gxn * gyn * gzn
    wg_ref[...] = total_of(part_y, "gy") * (1.0 / math.sqrt(cells))
    pending += ez + cz + cy + cx + ex + ey
    for c in pending:
        c.wait_send()


def local(dims, rho, vel, prs, ct, w_in, w_mid, w_out):
    gxn, gyn, gzn = dims
    zc, xc, yc = rho.shape
    reach = 40 // xc + 2
    if 2 * reach + 1 >= gxn:
        offsets = list(range(1, gxn - 1)) + [-1]
    else:
        offsets = list(range(1, reach + 1)) + list(range(-reach, 0))
    offsets = tuple(offsets)
    n_off = len(offsets)
    xfull, xadd = x_tables(xc, zc, gxn)
    feat = jnp.concatenate(
        [jnp.pad(w_in, ((0, 0), (0, 1))), jnp.asarray(np.eye(16, 10), F32)], 0
    )
    eye = jnp.asarray(np.eye(8), F32)
    w1 = (eye[:, None, None, :] * feat[None, :, :, None]).reshape(640, 80)
    w1 = jnp.concatenate([w1, w1, w1], 1)
    b1 = jnp.pad(w_in, ((0, 0), (0, 1))).T[:, None, None, :] * eye[None, :, :, None]
    b1 = b1.reshape(80, 512)
    b1 = jnp.concatenate([b1, b1, b1], 1)
    w2 = jnp.concatenate([w_mid, w_mid, w_mid], 1)
    w2t = jnp.concatenate([w_mid.T, w_mid.T, w_mid.T], 1)
    w3 = jnp.broadcast_to(w_out[:, None], (HID, 128))
    block = (16, 8, 128)
    n_sem = 2 * (n_off + 4) + (gxn - 1) + (gyn - 1) + (gzn - 1)
    vmem = pl.BlockSpec(memory_space=pltpu.VMEM)
    out = pl.pallas_call(
        functools.partial(kernel, dims, offsets),
        out_shape=(
            jax.ShapeDtypeStruct((5,) + block, F32),
            jax.ShapeDtypeStruct(block, F32),
            jax.ShapeDtypeStruct((3,) + block, F32),
            jax.ShapeDtypeStruct(block, F32),
            jax.ShapeDtypeStruct((HID, 128), F32),
        ),
        in_specs=[vmem] * 11,
        out_specs=(vmem,) * 5,
        scratch_shapes=[
            pltpu.VMEM((FIELDS,) + block, F32),
            pltpu.VMEM((FIELDS,) + block, F32),
            pltpu.VMEM((FIELDS,) + block, F32),
            pltpu.VMEM((FIELDS,) + block, F32),
            pltpu.VMEM((3, FIELDS) + block, F32),
            pltpu.VMEM((FIELDS,) + block, F32),
            pltpu.VMEM((640, 240), BF16),
            pltpu.VMEM((HID, 192), BF16),
            pltpu.VMEM((HID, 192), BF16),
            pltpu.VMEM((80, 1536), BF16),
            pltpu.VMEM((256, 256), F32),
            pltpu.VMEM((HID, 128), F32),
            pltpu.VMEM((2, 4, FIELDS, 8, 128), F32),
            pltpu.VMEM((2, n_off, 4, FIELDS, 8, 128), F32),
            pltpu.VMEM((2, 4, 8, 128), F32),
            pltpu.VMEM((2, 4, 8, 128), F32),
            pltpu.VMEM((2, 4, 8, 128), F32),
            pltpu.VMEM((2, 4, 8, 128), F32),
            pltpu.VMEM((2, FIELDS, 6, 8, 128), F32),
            pltpu.VMEM((2, FIELDS, 6, 8, 128), F32),
            pltpu.VMEM((gzn, HID, 128), F32),
            pltpu.VMEM((gxn, HID, 128), F32),
            pltpu.VMEM((gyn, HID, 128), F32),
            pltpu.SemaphoreType.DMA((n_sem,)),
            pltpu.SemaphoreType.DMA((n_sem,)),
        ],
        compiler_params=pltpu.CompilerParams(
            collective_id=0, has_side_effects=True, vmem_limit_bytes=40 * 1024 * 1024
        ),
    )(
        rho.reshape(block), vel.reshape((3,) + block), prs.reshape(block), ct.reshape((5,) + block),
        jnp.asarray(xfull), jnp.asarray(xadd), w1, w2, w2t, b1, w3,
    )
    nxt, arho, avel, aprs, wg = out
    return (
        nxt.reshape(ct.shape),
        arho.reshape(rho.shape),
        avel.reshape(vel.shape),
        aprs.reshape(prs.shape),
        wg[:, 64:73],
        wg[:, :64],
        wg[:, 80],
    )


def solution(mesh):
    dims = tuple(mesh.shape[axis] for axis in ("gx", "gy", "gz"))
    placed = (
        P("gz", "gx", "gy"),
        P(None, "gz", "gx", "gy"),
        P("gz", "gx", "gy"),
        P(None, "gz", "gx", "gy"),
        P(),
        P(),
        P(),
    )
    return jax.shard_map(
        functools.partial(local, dims),
        mesh=mesh,
        in_specs=placed,
        out_specs=(
            P(None, "gz", "gx", "gy"),
            P("gz", "gx", "gy"),
            P(None, "gz", "gx", "gy"),
            P("gz", "gx", "gy"),
            P(),
            P(),
            P(),
        ),
        check_vma=False,
    )
```

profile of v0, /device:TPU:0, one launch (start us, length us, event | category | flops | bytes accessed | tf_op | source)
XLA Modules:
  0.0 60.7 jit_solution(4951528800096419849)
XLA Ops:
  0.7 0.7 %pad_bitcast_fusion = (f32[10,64]{1,0:T(8,128)S(1)}, f32[64,10]{0,1:T(8,128)S(1)}) fusion(f32[64,9]{0,1:T(8,128)} %param.15), kind=kLoop, calls=%fused_computation.8 | loop fusion | bytes 7424 | tf_op jit(solution)/shard_map/transpose | solution.py:459
  1.4 0.1 pad_maximum_fusion.4
  1.5 0.6 copy-done.6
  2.1 0.1 copy.24
  2.2 0.1 pad_maximum_fusion.2
  2.3 0.6 copy-done.9
  2.9 0.1 broadcast_multiply_fusion.1
  3.0 0.1 mul.37
  3.2 0.2 copy.21
  3.3 0.5 copy-done.8
  3.8 0.1 broadcast_multiply_fusion
  3.9 0.1 mul.41
  4.2 0.3 pad_maximum_fusion.w1_ref
  4.5 0.6 copy-done
  5.2 0.1 copy-done.2
  5.2 50.8 %shard_map.162 = (f32[5,16,8,128]{3,2,1,0:T(8,128)S(1)}, f32[16,8,128]{2,1,0:T(8,128)S(1)}, f32[3,16,8,128]{3,2,1,0:T(8,128)S(1)}, f32[16,8,128]{2,1,0:T(8,128)S(1)}, f32[64,128]{1,0:T(8,128)S(1)}) custom-call(f32[16,8,128]{2,1,0:T(8,128)S(1)} %bitcast.23, f32[3,16,8,128]{3,2,1,0:T(8,128)S(1)} %bitcast.21, f32[16,8,128]{2,1,0:T(8,128)S(1)} %bitcast.24, ...), custom_call_target="tpu_custom_call" | custom-call | tf_op jit(solution)/shard_map/pallas_call | solution.py:468
  56.0 0.7 %slice_reduce_fusion = f32[64]{0:T(128)} fusion(f32[64,128]{1,0:T(8,128)S(1)} %get-tuple-element.16), kind=kLoop, calls=%fused_computation.6 | loop fusion | bytes 512 | tf_op jit(solution)/shard_map/slice | solution.py:521
  56.7 0.1 slice.9
  56.8 0.7 %copy.26 = f32[64,9]{0,1:T(8,128)} copy(f32[64,9]{1,0:T(8,128)S(1)} %slice.9) | data formatting | bytes 4608
  57.4 0.7 %copy.32 = f32[5,8,16,128]{3,2,1,0:T(8,128)} copy(f32[5,8,16,128]{3,2,1,0:T(8,128)S(1)} %bitcast.18) | data formatting | bytes 655360
  58.2 0.6 %copy.33 = f32[8,16,128]{2,1,0:T(8,128)} copy(f32[8,16,128]{2,1,0:T(8,128)S(1)} %bitcast.26) | data formatting | bytes 131072
  58.8 0.7 %copy.34 = f32[3,8,16,128]{3,2,1,0:T(8,128)} copy(f32[3,8,16,128]{3,2,1,0:T(8,128)S(1)} %bitcast.22) | data formatting | bytes 393216
  59.5 0.6 %copy.35 = f32[8,16,128]{2,1,0:T(8,128)} copy(f32[8,16,128]{2,1,0:T(8,128)S(1)} %bitcast.25) | data formatting | bytes 131072
  60.1 0.6 %copy.36 = f32[64,64]{1,0:T(8,128)} copy(f32[64,64]{1,0:T(8,128)S(1)} %bitcast.20) | data formatting | bytes 32768
  (19 shorter events, 0.2 us)
Async XLA Ops:
  0.6 0.7 %copy-start.7 = (f32[16,10]{0,1:T(8,128)S(1)}, f32[16,10]{0,1:T(8,128)}, u32[]{:S(2)}) copy-start(f32[16,10]{0,1:T(8,128)} %constant.11.clone) | copy-start | bytes 1924
  0.6 0.8 %copy-start.10 = (f32[64]{0:T(128)S(1)}, f32[64]{0:T(128)}, u32[]{:S(2)}) copy-start(f32[64]{0:T(128)} %param.17) | copy-start | bytes 772
  1.4 0.8 %copy-start.6 = (f32[64,64]{1,0:T(8,128)S(1)}, f32[64,64]{1,0:T(8,128)}, u32[]{:S(2)}) copy-start(f32[64,64]{1,0:T(8,128)} %param.16) | copy-start | bytes 49156
  2.2 0.7 %copy-start.9 = (f32[8,8]{0,1:T(8,128)S(1)}, f32[8,8]{0,1:T(8,128)}, u32[]{:S(2)}) copy-start(f32[8,8]{0,1:T(8,128)} %constant.12.clone) | copy-start | bytes 772
  3.1 0.7 %copy-start.8 = (f32[8,8]{1,0:T(8,128)S(1)}, f32[8,8]{1,0:T(8,128)}, u32[]{:S(2)}) copy-start(f32[8,8]{1,0:T(8,128)} %constant.17) | copy-start | bytes 772
  4.1 1.0 %copy-start = (f32[5,8,16,128]{3,2,1,0:T(8,128)S(1)}, f32[5,8,16,128]{3,2,1,0:T(8,128)}, u32[]{:S(2)}) copy-start(f32[5,8,16,128]{3,2,1,0:T(8,128)} %param.14) | copy-start | bytes 983044
  4.1 1.0 %copy-start.1 = (f32[3,8,16,128]{3,2,1,0:T(8,128)S(1)}, f32[3,8,16,128]{3,2,1,0:T(8,128)}, u32[]{:S(2)}) copy-start(f32[3,8,16,128]{3,2,1,0:T(8,128)} %param.12) | copy-start | bytes 589828
  4.2 1.1 %copy-start.2 = (bf16[160,384]{1,0:T(8,128)(2,1)S(1)}, bf16[160,384]{1,0:T(8,128)(2,1)}, u32[]{:S(2)}) copy-start(bf16[160,384]{1,0:T(8,128)(2,1)} %constant.13.clone.xfull_ref) | copy-start | bytes 368644
  4.2 1.1 %copy-start.3 = (f32[8,16,128]{2,1,0:T(8,128)S(1)}, f32[8,16,128]{2,1,0:T(8,128)}, u32[]{:S(2)}) copy-start(f32[8,16,128]{2,1,0:T(8,128)} %param.11) | copy-start | bytes 196612
  4.2 1.1 %copy-start.4 = (f32[8,16,128]{2,1,0:T(8,128)S(1)}, f32[8,16,128]{2,1,0:T(8,128)}, u32[]{:S(2)}) copy-start(f32[8,16,128]{2,1,0:T(8,128)} %param.13) | copy-start | bytes 196612
  4.2 1.0 %copy-start.5 = (bf16[128,96]{1,0:T(8,128)(2,1)S(1)}, bf16[128,96]{1,0:T(8,128)(2,1)}, u32[]{:S(2)}) copy-start(bf16[128,96]{1,0:T(8,128)(2,1)} %constant.14.clone.xadd_ref) | copy-start | bytes 73732
where the time goes:
time: 61.1 us; the launch traced here: 60.7 us
  Pallas kernels  50.8 us (83%)
  local copies, waits for them, and re-layouts  8.46 us (14%)
  between operations  0.78 us (1%)
  other arithmetic  0.72 us (1%)
    pallas_call x1, Pallas kernels, local(): pl.pallas_call(functools.partial(kernel, dims, offsets), out_shape=(jax.S...  50.8 us
    unnamed x29, local copies, waits for them, and re-layouts  6.47 us

commit v1 on v0

--- a/solution.py
+++ b/solution.py
@@ -118,7 +118,7 @@
         b = remote(src.at[:, 0:6], zhi.at[ph], "gz", -1)
         return [a, b]
 
-    def send_y(ph, src):
+    def pack_y(ph, src):
         for j in range(FIELDS):
             for q in range(4):
                 block = src[j, 4 * q : 4 * q + 4]
@@ -136,12 +136,14 @@
                     ]
         ypl[ph] = keep[0]
         ypr[ph] = keep[1]
+
+    def start_y(ph):
         return [
             remote(ypl.at[ph], yl.at[ph], "gy", 1),
             remote(ypr.at[ph], yr.at[ph], "gy", -1),
         ]
 
-    def send_x(ph, src, put):
+    def solve_x(ph, src, put):
         def one(j, carry):
             y = jnp.dot(
                 xfull_ref[...], stack3(src[j].reshape(128, 128)), preferred_element_type=F32
@@ -151,7 +153,9 @@
                 mom[ph, m, j] = y[128 + 8 * m : 136 + 8 * m]
             return carry
 
-        lax.fori_loop(0, FIELDS, one, 0, unroll=3)
+        lax.fori_loop(0, FIELDS, one, 0, unroll=9)
+
+    def start_x(ph):
         copies = []
         for slot, offset in enumerate(offsets):
             lo = 0 if offset == 1 else 1
@@ -218,19 +222,21 @@
             add(j, y.reshape(16, 8, 128))
             return carry
 
-        lax.fori_loop(0, FIELDS, one, 0, unroll=3)
+        lax.fori_loop(0, FIELDS, one, 0, unroll=9)
 
     f0[0:3] = vel_ref[...]
     f0[3] = prs_ref[...] / rho_ref[...]
     f0[4:9] = ct_ref[...]
-    pl.semaphore_wait(barrier, total)
-    cz = send_z(0, f0)
-    cy = send_y(0, f0)
 
     def put0(j, value):
         der[0, j] = value
 
-    cx = send_x(0, f0, put0)
+    solve_x(0, f0, put0)
+    pl.semaphore_wait(barrier, total)
+    cx = start_x(0)
+    cz = send_z(0, f0)
+    pack_y(0, f0)
+    cy = start_y(0)
     pending += cz + cy + cx
 
     def halves(src, dst, third):
@@ -368,7 +374,7 @@
         )
         return carry
 
-    lax.fori_loop(0, 16, group, 0)
+    lax.fori_loop(0, 16, group, 0, unroll=2)
 
     wlane = lax.broadcasted_iota(jnp.int32, (HID, 128), 1)
     mid_w = acc[0:64, 0:128] + acc[64:128, 0:128] + pltpu.roll(acc[0:64, 0:128], 64, 1)
@@ -393,14 +399,15 @@
             value = value + buf[i]
         return value
 
-    ez = exchange(part_z, "gz", mine)
-    cz = send_z(1, fz)
-    cy = send_y(1, fy)
-
     def put1(j, value):
         back[j] = value
 
-    cx = send_x(1, fx, put1)
+    solve_x(1, fx, put1)
+    cx = start_x(1)
+    cz = send_z(1, fz)
+    ez = exchange(part_z, "gz", mine)
+    pack_y(1, fy)
+    cy = start_y(1)
     for c in ez:
         c.wait_recv()
     ex = exchange(part_x, "gx", total_of(part_z, "gz"))

time: 61.1 us -> 56 us (0.917)
  Pallas kernels: 50.8 us -> 45.7 us
    pallas_call x1, Pallas kernels: 50.8 us -> 45.7 us  [local(): pl.pallas_call(functools.partial(kernel, dims, offsets), out_shape=(jax.S...]
where the time goes in v1:
time: 56 us; the launch traced here: 55.6 us
  Pallas kernels  45.7 us (82%)
  local copies, waits for them, and re-layouts  8.46 us (15%)
  between operations  0.78 us (1%)
  other arithmetic  0.72 us (1%)
    pallas_call x1, Pallas kernels, local(): pl.pallas_call(functools.partial(kernel, dims, offsets), out_shape=(jax.S...  45.7 us
    unnamed x29, local copies, waits for them, and re-layouts  6.47 us

profile of v1, /device:TPU:0, one launch (start us, length us, event | category | flops | bytes accessed | tf_op | source)
XLA Modules:
  0.0 55.6 jit_solution(13702902320591598450)
XLA Ops:
  0.7 0.7 %pad_bitcast_fusion = (f32[10,64]{1,0:T(8,128)S(1)}, f32[64,10]{0,1:T(8,128)S(1)}) fusion(f32[64,9]{0,1:T(8,128)} %param.15), kind=kLoop, calls=%fused_computation.8 | loop fusion | bytes 7424 | tf_op jit(solution)/shard_map/transpose | solution.py:466
  1.4 0.1 pad_maximum_fusion.4
  1.5 0.6 %copy-done.6 = f32[64,64]{1,0:T(8,128)S(1)} copy-done((f32[64,64]{1,0:T(8,128)S(1)}, f32[64,64]{1,0:T(8,128)}, u32[]{:S(2)}) %copy-start.6) | copy-done | bytes 16408
  2.1 0.1 copy.24
  2.2 0.1 pad_maximum_fusion.2
  2.3 0.6 %copy-done.9 = f32[8,8]{0,1:T(8,128)S(1)} copy-done((f32[8,8]{0,1:T(8,128)S(1)}, f32[8,8]{0,1:T(8,128)}, u32[]{:S(2)}) %copy-start.9) | copy-done | bytes 280
  2.9 0.1 broadcast_multiply_fusion.1
  3.0 0.1 mul.37
  3.2 0.2 copy.21
  3.3 0.5 copy-done.8
  3.8 0.1 broadcast_multiply_fusion
  3.9 0.1 mul.41
  4.2 0.3 pad_maximum_fusion.w1_ref
  4.5 0.6 %copy-done = f32[5,8,16,128]{3,2,1,0:T(8,128)S(1)} copy-done((f32[5,8,16,128]{3,2,1,0:T(8,128)S(1)}, f32[5,8,16,128]{3,2,1,0:T(8,128)}, u32[]{:S(2)}) %copy-start) | copy-done | bytes 327704
  5.2 0.1 copy-done.2
  5.2 45.7 %shard_map.162 = (f32[5,16,8,128]{3,2,1,0:T(8,128)S(1)}, f32[16,8,128]{2,1,0:T(8,128)S(1)}, f32[3,16,8,128]{3,2,1,0:T(8,128)S(1)}, f32[16,8,128]{2,1,0:T(8,128)S(1)}, f32[64,128]{1,0:T(8,128)S(1)}) custom-call(f32[16,8,128]{2,1,0:T(8,128)S(1)} %bitcast.23, f32[3,16,8,128]{3,2,1,0:T(8,128)S(1)} %bitcast.21, f32[16,8,128]{2,1,0:T(8,128)S(1)} %bitcast.24, ...), custom_call_target="tpu_custom_call" | custom-call | tf_op jit(solution)/shard_map/pallas_call | solution.py:475
  50.9 0.7 %slice_reduce_fusion = f32[64]{0:T(128)} fusion(f32[64,128]{1,0:T(8,128)S(1)} %get-tuple-element.16), kind=kLoop, calls=%fused_computation.6 | loop fusion | bytes 512 | tf_op jit(solution)/shard_map/slice | solution.py:528
  51.6 0.1 slice.9
  51.7 0.7 %copy.26 = f32[64,9]{0,1:T(8,128)} copy(f32[64,9]{1,0:T(8,128)S(1)} %slice.9) | data formatting | bytes 4608
  52.3 0.7 %copy.32 = f32[5,8,16,128]{3,2,1,0:T(8,128)} copy(f32[5,8,16,128]{3,2,1,0:T(8,128)S(1)} %bitcast.18) | data formatting | bytes 655360
  53.1 0.6 %copy.33 = f32[8,16,128]{2,1,0:T(8,128)} copy(f32[8,16,128]{2,1,0:T(8,128)S(1)} %bitcast.26) | data formatting | bytes 131072
  53.7 0.7 %copy.34 = f32[3,8,16,128]{3,2,1,0:T(8,128)} copy(f32[3,8,16,128]{3,2,1,0:T(8,128)S(1)} %bitcast.22) | data formatting | bytes 393216
  54.4 0.6 %copy.35 = f32[8,16,128]{2,1,0:T(8,128)} copy(f32[8,16,128]{2,1,0:T(8,128)S(1)} %bitcast.25) | data formatting | bytes 131072
  55.0 0.6 %copy.36 = f32[64,64]{1,0:T(8,128)} copy(f32[64,64]{1,0:T(8,128)S(1)} %bitcast.20) | data formatting | bytes 32768
  (19 shorter events, 0.2 us)
Async XLA Ops:
  0.6 0.7 %copy-start.7 = (f32[16,10]{0,1:T(8,128)S(1)}, f32[16,10]{0,1:T(8,128)}, u32[]{:S(2)}) copy-start(f32[16,10]{0,1:T(8,128)} %constant.11.clone) | copy-start | bytes 1924
  0.6 0.8 %copy-start.10 = (f32[64]{0:T(128)S(1)}, f32[64]{0:T(128)}, u32[]{:S(2)}) copy-start(f32[64]{0:T(128)} %param.17) | copy-start | bytes 772
  1.4 0.8 %copy-start.6 = (f32[64,64]{1,0:T(8,128)S(1)}, f32[64,64]{1,0:T(8,128)}, u32[]{:S(2)}) copy-start(f32[64,64]{1,0:T(8,128)} %param.16) | copy-start | bytes 49156
  2.2 0.7 %copy-start.9 = (f32[8,8]{0,1:T(8,128)S(1)}, f32[8,8]{0,1:T(8,128)}, u32[]{:S(2)}) copy-start(f32[8,8]{0,1:T(8,128)} %constant.12.clone) | copy-start | bytes 772
  3.1 0.7 %copy-start.8 = (f32[8,8]{1,0:T(8,128)S(1)}, f32[8,8]{1,0:T(8,128)}, u32[]{:S(2)}) copy-start(f32[8,8]{1,0:T(8,128)} %constant.17) | copy-start | bytes 772
  4.1 1.0 %copy-start = (f32[5,8,16,128]{3,2,1,0:T(8,128)S(1)}, f32[5,8,16,128]{3,2,1,0:T(8,128)}, u32[]{:S(2)}) copy-start(f32[5,8,16,128]{3,2,1,0:T(8,128)} %param.14) | copy-start | bytes 983044
  4.1 1.0 %copy-start.1 = (f32[3,8,16,128]{3,2,1,0:T(8,128)S(1)}, f32[3,8,16,128]{3,2,1,0:T(8,128)}, u32[]{:S(2)}) copy-start(f32[3,8,16,128]{3,2,1,0:T(8,128)} %param.12) | copy-start | bytes 589828
  4.2 1.1 %copy-start.2 = (bf16[160,384]{1,0:T(8,128)(2,1)S(1)}, bf16[160,384]{1,0:T(8,128)(2,1)}, u32[]{:S(2)}) copy-start(bf16[160,384]{1,0:T(8,128)(2,1)} %constant.13.clone.xfull_ref) | copy-start | bytes 368644
  4.2 1.1 %copy-start.3 = (f32[8,16,128]{2,1,0:T(8,128)S(1)}, f32[8,16,128]{2,1,0:T(8,128)}, u32[]{:S(2)}) copy-start(f32[8,16,128]{2,1,0:T(8,128)} %param.11) | copy-start | bytes 196612
  4.2 1.1 %copy-start.4 = (f32[8,16,128]{2,1,0:T(8,128)S(1)}, f32[8,16,128]{2,1,0:T(8,128)}, u32[]{:S(2)}) copy-start(f32[8,16,128]{2,1,0:T(8,128)} %param.13) | copy-start | bytes 196612
  4.2 1.0 %copy-start.5 = (bf16[128,96]{1,0:T(8,128)(2,1)S(1)}, bf16[128,96]{1,0:T(8,128)(2,1)}, u32[]{:S(2)}) copy-start(bf16[128,96]{1,0:T(8,128)(2,1)} %constant.14.clone.xadd_ref) | copy-start | bytes 73732

commit v2 on v1

--- a/solution.py
+++ b/solution.py
@@ -232,10 +232,10 @@
         der[0, j] = value
 
     solve_x(0, f0, put0)
+    pack_y(0, f0)
     pl.semaphore_wait(barrier, total)
     cx = start_x(0)
     cz = send_z(0, f0)
-    pack_y(0, f0)
     cy = start_y(0)
     pending += cz + cy + cx
 
@@ -249,7 +249,10 @@
     halves(w1_ref, w1s, 80)
     halves(w2_ref, w2s, HID)
     halves(w2t_ref, w2ts, HID)
-    halves(b1_ref, b1s, 8 * HID)
+    b1_hi, b1_lo = split(b1_ref[...])
+    b1s[:, 0:512] = b1_hi
+    b1s[:, 512:1024] = b1_lo
+    b1s[:, 1024:1536] = b1_hi
     acc[...] = jnp.zeros_like(acc)
     w3acc[...] = jnp.zeros_like(w3acc)
 
@@ -374,7 +377,7 @@
         )
         return carry
 
-    lax.fori_loop(0, 16, group, 0, unroll=2)
+    lax.fori_loop(0, 16, group, 0, unroll=4)
 
     wlane = lax.broadcasted_iota(jnp.int32, (HID, 128), 1)
     mid_w = acc[0:64, 0:128] + acc[64:128, 0:128] + pltpu.roll(acc[0:64, 0:128], 64, 1)
@@ -465,7 +468,6 @@
     w1 = jnp.concatenate([w1, w1, w1], 1)
     b1 = jnp.pad(w_in, ((0, 0), (0, 1))).T[:, None, None, :] * eye[None, :, :, None]
     b1 = b1.reshape(80, 512)
-    b1 = jnp.concatenate([b1, b1, b1], 1)
     w2 = jnp.concatenate([w_mid, w_mid, w_mid], 1)
     w2t = jnp.concatenate([w_mid.T, w_mid.T, w_mid.T], 1)
     w3 = jnp.broadcast_to(w_out[:, None], (HID, 128))

time: 56 us -> 55.3 us (0.987)
  Pallas kernels: 45.7 us -> 45 us
    pallas_call x1, Pallas kernels: 45.7 us -> 45 us  [local(): pl.pallas_call(functools.partial(kernel, dims, offsets), out_shape=(jax.S...]
where the time goes in v2:
time: 55.3 us; the launch traced here: 54.9 us
  Pallas kernels  45 us (81%)
  local copies, waits for them, and re-layouts  8.46 us (15%)
  between operations  0.78 us (1%)
  other arithmetic  0.68 us (1%)
    pallas_call x1, Pallas kernels, local(): pl.pallas_call(functools.partial(kernel, dims, offsets), out_shape=(jax.S...  45 us
    unnamed x29, local copies, waits for them, and re-layouts  6.47 us

profile of v2, /device:TPU:0, one launch (start us, length us, event | category | flops | bytes accessed | tf_op | source)
XLA Modules:
  0.0 54.9 jit_solution(3969737554317771555)
XLA Ops:
  0.7 0.7 %pad_bitcast_fusion = (f32[10,64]{1,0:T(8,128)S(1)}, f32[64,10]{0,1:T(8,128)S(1)}) fusion(f32[64,9]{0,1:T(8,128)} %param.15), kind=kLoop, calls=%fused_computation.7 | loop fusion | bytes 7424 | tf_op jit(solution)/shard_map/transpose | solution.py:469
  1.4 0.1 pad_maximum_fusion.3
  1.5 0.6 %copy-done.6 = f32[64,64]{1,0:T(8,128)S(1)} copy-done((f32[64,64]{1,0:T(8,128)S(1)}, f32[64,64]{1,0:T(8,128)}, u32[]{:S(2)}) %copy-start.6) | copy-done | bytes 16408
  2.1 0.1 copy.24
  2.2 0.1 pad_maximum_fusion.1
  2.3 0.6 %copy-done.9 = f32[8,8]{0,1:T(8,128)S(1)} copy-done((f32[8,8]{0,1:T(8,128)S(1)}, f32[8,8]{0,1:T(8,128)}, u32[]{:S(2)}) %copy-start.9) | copy-done | bytes 280
  2.9 0.1 broadcast_multiply_fusion.1
  3.0 0.1 mul.37
  3.2 0.2 copy.21
  3.3 0.5 copy-done.8
  3.8 0.1 broadcast_multiply_fusion
  3.9 0.1 mul.41.b1_ref
  4.1 0.3 pad_maximum_fusion.w1_ref
  4.5 0.6 %copy-done = f32[5,8,16,128]{3,2,1,0:T(8,128)S(1)} copy-done((f32[5,8,16,128]{3,2,1,0:T(8,128)S(1)}, f32[5,8,16,128]{3,2,1,0:T(8,128)}, u32[]{:S(2)}) %copy-start) | copy-done | bytes 327704
  5.1 0.1 copy-done.2
  5.2 45.0 %shard_map.162 = (f32[5,16,8,128]{3,2,1,0:T(8,128)S(1)}, f32[16,8,128]{2,1,0:T(8,128)S(1)}, f32[3,16,8,128]{3,2,1,0:T(8,128)S(1)}, f32[16,8,128]{2,1,0:T(8,128)S(1)}, f32[64,128]{1,0:T(8,128)S(1)}) custom-call(f32[16,8,128]{2,1,0:T(8,128)S(1)} %bitcast.23, f32[3,16,8,128]{3,2,1,0:T(8,128)S(1)} %bitcast.21, f32[16,8,128]{2,1,0:T(8,128)S(1)} %bitcast.24, ...), custom_call_target="tpu_custom_call" | custom-call | tf_op jit(solution)/shard_map/pallas_call | solution.py:477
  50.2 0.7 %slice_reduce_fusion = f32[64]{0:T(128)} fusion(f32[64,128]{1,0:T(8,128)S(1)} %get-tuple-element.16), kind=kLoop, calls=%fused_computation.5 | loop fusion | bytes 512 | tf_op jit(solution)/shard_map/slice | solution.py:530
  50.9 0.1 slice.9
  51.0 0.7 %copy.26 = f32[64,9]{0,1:T(8,128)} copy(f32[64,9]{1,0:T(8,128)S(1)} %slice.9) | data formatting | bytes 4608
  51.7 0.7 %copy.32 = f32[5,8,16,128]{3,2,1,0:T(8,128)} copy(f32[5,8,16,128]{3,2,1,0:T(8,128)S(1)} %bitcast.19) | data formatting | bytes 655360
  52.4 0.6 %copy.33 = f32[8,16,128]{2,1,0:T(8,128)} copy(f32[8,16,128]{2,1,0:T(8,128)S(1)} %bitcast.26) | data formatting | bytes 131072
  53.0 0.7 %copy.34 = f32[3,8,16,128]{3,2,1,0:T(8,128)} copy(f32[3,8,16,128]{3,2,1,0:T(8,128)S(1)} %bitcast.22) | data formatting | bytes 393216
  53.7 0.6 %copy.35 = f32[8,16,128]{2,1,0:T(8,128)} copy(f32[8,16,128]{2,1,0:T(8,128)S(1)} %bitcast.25) | data formatting | bytes 131072
  54.3 0.6 %copy.36 = f32[64,64]{1,0:T(8,128)} copy(f32[64,64]{1,0:T(8,128)S(1)} %bitcast.20) | data formatting | bytes 32768
  (18 shorter events, 0.2 us)
Async XLA Ops:
  0.6 0.7 %copy-start.7 = (f32[16,10]{0,1:T(8,128)S(1)}, f32[16,10]{0,1:T(8,128)}, u32[]{:S(2)}) copy-start(f32[16,10]{0,1:T(8,128)} %constant.11.clone) | copy-start | bytes 1924
  0.6 0.8 %copy-start.10 = (f32[64]{0:T(128)S(1)}, f32[64]{0:T(128)}, u32[]{:S(2)}) copy-start(f32[64]{0:T(128)} %param.17) | copy-start | bytes 772
  1.4 0.8 %copy-start.6 = (f32[64,64]{1,0:T(8,128)S(1)}, f32[64,64]{1,0:T(8,128)}, u32[]{:S(2)}) copy-start(f32[64,64]{1,0:T(8,128)} %param.16) | copy-start | bytes 49156
  2.2 0.7 %copy-start.9 = (f32[8,8]{0,1:T(8,128)S(1)}, f32[8,8]{0,1:T(8,128)}, u32[]{:S(2)}) copy-start(f32[8,8]{0,1:T(8,128)} %constant.12.clone) | copy-start | bytes 772
  3.1 0.7 %copy-start.8 = (f32[8,8]{1,0:T(8,128)S(1)}, f32[8,8]{1,0:T(8,128)}, u32[]{:S(2)}) copy-start(f32[8,8]{1,0:T(8,128)} %constant.17) | copy-start | bytes 772
  4.1 1.0 %copy-start = (f32[5,8,16,128]{3,2,1,0:T(8,128)S(1)}, f32[5,8,16,128]{3,2,1,0:T(8,128)}, u32[]{:S(2)}) copy-start(f32[5,8,16,128]{3,2,1,0:T(8,128)} %param.14) | copy-start | bytes 983044
  4.1 1.0 %copy-start.1 = (f32[3,8,16,128]{3,2,1,0:T(8,128)S(1)}, f32[3,8,16,128]{3,2,1,0:T(8,128)}, u32[]{:S(2)}) copy-start(f32[3,8,16,128]{3,2,1,0:T(8,128)} %param.12) | copy-start | bytes 589828
  4.1 1.1 %copy-start.2 = (bf16[160,384]{1,0:T(8,128)(2,1)S(1)}, bf16[160,384]{1,0:T(8,128)(2,1)}, u32[]{:S(2)}) copy-start(bf16[160,384]{1,0:T(8,128)(2,1)} %constant.13.clone.xfull_ref) | copy-start | bytes 368644
  4.1 1.1 %copy-start.3 = (f32[8,16,128]{2,1,0:T(8,128)S(1)}, f32[8,16,128]{2,1,0:T(8,128)}, u32[]{:S(2)}) copy-start(f32[8,16,128]{2,1,0:T(8,128)} %param.11) | copy-start | bytes 196612
  4.1 1.1 %copy-start.4 = (f32[8,16,128]{2,1,0:T(8,128)S(1)}, f32[8,16,128]{2,1,0:T(8,128)}, u32[]{:S(2)}) copy-start(f32[8,16,128]{2,1,0:T(8,128)} %param.13) | copy-start | bytes 196612
  4.1 1.0 %copy-start.5 = (bf16[128,96]{1,0:T(8,128)(2,1)S(1)}, bf16[128,96]{1,0:T(8,128)(2,1)}, u32[]{:S(2)}) copy-start(bf16[128,96]{1,0:T(8,128)(2,1)} %constant.14.clone.xadd_ref) | copy-start | bytes 73732
